TPU v7x, 512 devices: a whole 4x8x8 slice. The times are simulated.
512 devices in a mesh: dp: 8 (over y), ta: 16 (over z_lo, x), ha: 4 (over z_hi, core).
Axes of the slice: x: 4, y: 8, z: 8 (z_hi: 2, z_lo: 4; z = z_hi * 4 + z_lo), core: 2. Of those that a mesh axis runs over, the one named last changes fastest.
Arguments:
- decoder_feature_rows: bfloat16 [32768, 768], P(('dp', 'ta', 'ha')), parts along dimension 0, may hold values from -12 to 12
- slot_row_index: int32 [32768], P('dp'), parts along dimension 0, may hold values from 0 to 4095, as said below
- latent_frame_count: int32 [48], P('dp'), parts along dimension 0, may hold values from 1 to 81, 256 in all
- first_norm_gain: float32 [384], replicated, may hold values from 0.1 to 1.9
- first_norm_bias: float32 [384], replicated, may hold values from -3 to 3
- first_convolution_weight: bfloat16 [3, 3, 3, 384, 384], P(None, None, None, 'ha'), may hold values from -0.0625 to 0.0625
- first_convolution_bias: float32 [384], replicated, may hold values from -3 to 3
- second_norm_gain: float32 [384], replicated, may hold values from 0.1 to 1.9
- second_norm_bias: float32 [384], replicated, may hold values from -3 to 3
- second_convolution_weight: bfloat16 [3, 3, 3, 384, 384], P(None, None, None, 'ha'), may hold values from -0.0625 to 0.0625
- second_convolution_bias: float32 [384], replicated, may hold values from -3 to 3
Outputs:
- decoded: bfloat16 [2048, 16, 2, 384], P(('dp', 'ta'), 'ha'), parts along dimension 0
There are 8 independent parts, one for each index of `dp`. A program takes and returns all parts, laid end to end along the dimension named above; an argument that names none is the same for every part. Nothing has to cross between parts.
Inputs may be any that keep to these rules, and one draw needn't show every extreme that they name: `slot_row_index`: A permutation of 0 to 4095. Slot i lies on the device of flat index i // 64 over ta+ha; row g is owned by the device of ta index (g // 16) // 16 and ha index (g % 16) // 4. The slots of one device hold at most 2 rows of any one owner, and exactly 2 of some owner.
All inputs are finite; a program needn't handle non-finite values.
Results may differ from a plain program's by a relative error of at most 0.0042.
Values may be sent and summed in bfloat16 or wider, within the bound.
No kernel may reach another device: no remote copies, remote signals or barrier semaphores. Data moves between devices by JAX's collectives and lax.ppermute only.
A program may use at most 64 MiB of HBM per device.

v0:
```python
import jax
import jax.numpy as jnp
from jax import lax
from jax.sharding import PartitionSpec as P

CH = 384
GROUPS = 32
F_DEV = 16
R_DEV = 4
COLS = 2


def from_behind(value, axis, by):
    length = lax.axis_size(axis)
    pairs = [(i, i + by) for i in range(length) if 0 <= i + by < length]
    return lax.ppermute(value, axis, pairs)


def group_sums(values, groups):
    extent = values.shape
    grouped = values.reshape(extent[0], extent[1] * extent[2], groups, extent[3] // groups)
    return (jnp.sum(grouped, axis=(1, 3)), jnp.sum(grouped * grouped, axis=(1, 3)))


def normalize(values, totals, squares, entries, gain_vec, offset, groups):
    average = totals / entries
    spread = squares / entries - average * average
    inverse = lax.rsqrt(spread + 1e-06)
    extent = values.shape
    grouped = values.reshape(extent[0], extent[1], extent[2], groups, extent[3] // groups)
    centred = (grouped - average[:, None, None, :, None]) * inverse[:, None, None, :, None]
    scaled = centred.reshape(extent) * gain_vec + offset
    return jax.nn.silu(scaled).astype(jnp.bfloat16)


def extend_frames(values):
    earlier = from_behind(values[-2:], "ta", 1)
    return jnp.concatenate([earlier, values], axis=0)


def whole_rows(values):
    return lax.all_gather(values, "ha", axis=1, tiled=True)


def shared_norm(values, gain_vec, offset, entries):
    part_sums, part_squares = group_sums(values, GROUPS)
    totals, squares = lax.psum((part_sums, part_squares), "ha")
    return normalize(values, totals, squares, entries, gain_vec, offset, GROUPS)


def causal_conv(extended, weight, masks):
    frames = extended.shape[0] - 2
    image_height = extended.shape[1]
    columns = extended.shape[2]
    channels = extended.shape[3]
    outputs = weight.shape[3]
    padded = jnp.pad(extended, ((0, 0), (1, 1), (1, 1), (0, 0)))
    stacked = jnp.concatenate(
        [
            padded[time_tap : time_tap + frames] * masks[time_tap][:, None, None, None]
            for time_tap in range(3)
        ],
        axis=3,
    )
    kernel = jnp.transpose(weight, (0, 4, 1, 2, 3)).reshape(3 * channels, 9 * outputs)
    taps = jnp.dot(stacked.reshape(-1, 3 * channels), kernel, preferred_element_type=jnp.float32)
    taps = taps.reshape(frames, image_height + 2, columns + 2, 9, outputs)
    total = jnp.zeros((frames, image_height, columns, outputs), jnp.float32)
    for row_tap in range(3):
        for col_tap in range(3):
            total = (
                total
                + taps[
                    :,
                    row_tap : row_tap + image_height,
                    col_tap : col_tap + columns,
                    3 * row_tap + col_tap,
                ]
            )
    return total


def rearrange_rows(decoder_feature_rows, slot_row_index, image_height):
    devices = lax.axis_size(("ta", "ha"))
    ha_count = lax.axis_size("ha")
    number_of_slots = decoder_feature_rows.shape[0]
    capacity = number_of_slots // devices + 1
    own_index = lax.axis_index(("ta", "ha"))
    plan_grid = slot_row_index.reshape(devices, number_of_slots)
    frame_of = plan_grid // image_height
    row_in = plan_grid % image_height
    owners = frame_of // F_DEV * ha_count + row_in // R_DEV
    places = frame_of % F_DEV * R_DEV + row_in % R_DEV
    my_owners = lax.dynamic_slice_in_dim(owners, own_index, 1, 0)[0]
    matches = (my_owners[:, None] == jnp.arange(devices, dtype=jnp.int32)[None, :]).astype(
        jnp.int32
    )
    ranking = jnp.sum((jnp.cumsum(matches, axis=0) - 1) * matches, axis=1)
    position = my_owners * capacity + ranking
    row_packing = (
        jnp.arange(devices * capacity, dtype=jnp.int32)[:, None] == position[None, :]
    ).astype(jnp.bfloat16)
    departing_rows = jnp.dot(
        row_packing, decoder_feature_rows, preferred_element_type=jnp.float32
    ).astype(jnp.bfloat16)
    incoming = lax.all_to_all(
        departing_rows.reshape(devices, capacity, -1),
        ("ta", "ha"),
        split_axis=0,
        concat_axis=0,
        tiled=True,
    )
    arrivals = (owners == own_index).astype(jnp.int32)
    order_in = jnp.cumsum(arrivals, axis=1) - 1
    chosen = arrivals[:, None, :] * (
        order_in[:, None, :] == jnp.arange(capacity, dtype=jnp.int32)[None, :, None]
    ).astype(jnp.int32)
    filled = jnp.sum(chosen, axis=2)
    target = jnp.sum(chosen * places[:, None, :], axis=2) + filled - 1
    unpack = (
        jnp.arange(number_of_slots, dtype=jnp.int32)[:, None] == target.reshape(1, -1)
    ).astype(jnp.bfloat16)
    placed = jnp.dot(
        unpack, incoming.reshape(devices * capacity, -1), preferred_element_type=jnp.float32
    )
    return placed.astype(jnp.bfloat16).reshape(F_DEV, R_DEV, COLS, CH)


def local(
    decoder_feature_rows,
    slot_row_index,
    latent_frame_count,
    first_norm_gain,
    first_norm_bias,
    first_convolution_weight,
    first_convolution_bias,
    second_norm_gain,
    second_norm_bias,
    second_convolution_weight,
    second_convolution_bias,
):
    ha_count = lax.axis_size("ha")
    ha_index = lax.axis_index("ha")
    image_height = R_DEV * ha_count
    out_width = CH // ha_count
    latent_row_list = rearrange_rows(decoder_feature_rows, slot_row_index, image_height)
    frame_ids = lax.axis_index("ta") * F_DEV + jnp.arange(F_DEV, dtype=jnp.int32)
    video_ends = jnp.cumsum(latent_frame_count)
    starts = jnp.sum(
        jnp.where(video_ends[None, :] <= frame_ids[:, None], latent_frame_count[None, :], 0), axis=1
    )
    masks = jnp.stack([frame_ids - 2 + time_tap >= starts for time_tap in range(3)]).astype(
        jnp.bfloat16
    )
    bias_first = lax.dynamic_slice_in_dim(first_convolution_bias, ha_index * out_width, out_width)
    bias_second = lax.dynamic_slice_in_dim(second_convolution_bias, ha_index * out_width, out_width)
    entries = image_height * COLS * (CH // GROUPS)
    latent_float = latent_row_list.astype(jnp.float32)
    first_act = shared_norm(latent_float, first_norm_gain, first_norm_bias, entries)
    hidden = (
        causal_conv(whole_rows(extend_frames(first_act)), first_convolution_weight, masks)
        + bias_first
    ).astype(jnp.bfloat16)
    hidden_rows = lax.all_to_all(hidden, "ha", split_axis=1, concat_axis=3, tiled=True)
    second_act = shared_norm(
        hidden_rows.astype(jnp.float32), second_norm_gain, second_norm_bias, entries
    )
    result = (
        causal_conv(whole_rows(extend_frames(second_act)), second_convolution_weight, masks)
        + bias_second
    )
    output_rows = lax.all_to_all(result, "ha", split_axis=1, concat_axis=3, tiled=True)
    return (output_rows + latent_float).astype(jnp.bfloat16)


def solution(mesh):
    in_specs = (
        P(("dp", "ta", "ha"), None),
        P("dp"),
        P("dp"),
        P(),
        P(),
        P(None, None, None, "ha", None),
        P(),
        P(),
        P(),
        P(None, None, None, "ha", None),
        P(),
    )
    out_specs = P(("dp", "ta"), "ha", None, None)
    return jax.shard_map(local, mesh=mesh, in_specs=in_specs, out_specs=out_specs, check_vma=False)
```

profile of v0, /device:TPU:112, one launch (start us, length us, event | category | flops | bytes accessed | tf_op | source)
XLA Modules:
  0.0 152.8 jit_solution(9828036770972007920)
XLA Ops:
  0.0 0.8 reshape.350
  1.5 0.8 reshape.351
  2.2 13.0 %all-to-all-start = ((bf16[64,2,768]{2,1,0:T(2,128)(2,1)}), bf16[64,2,768]{2,1,0:T(2,128)(2,1)S(1)}, u32[]{:S(2)}, u32[]{:S(2)}) async-start(bf16[64,2,768]{2,1,0:T(2,128)(2,1)} %reshape.351), calls=%async_computation | async-start | bytes 393216 | tf_op jit(solution)/shard_map/all_to_all | solution.py:106
  15.2 0.2 reduce_window_sum.29
  15.6 0.8 reduce-window.8
  16.5 0.7 select_reduce_fusion.2
  17.6 9.4 %all-to-all-done = bf16[64,2,768]{2,1,0:T(2,128)(2,1)S(1)} async-done(((bf16[64,2,768]{2,1,0:T(2,128)(2,1)}), bf16[64,2,768]{2,1,0:T(2,128)(2,1)S(1)}, u32[]{:S(2)}, u32[]{:S(2)}) %all-to-all-start) | async-done | bytes 196640 | tf_op jit(solution)/shard_map/all_to_all | solution.py:106
  27.2 2.3 %reshape.358 = f32[16,8,32,12]{3,2,1,0:T(8,128)S(1)} reshape(f32[64,768]{1,0:T(8,128)S(1)} %fusion.16) | data formatting | bytes 393216 | tf_op jit(solution)/shard_map/convert_element_type | solution.py:158
  29.7 0.4 fusion.44
  30.1 19.1 %all-reduce.3 = (f32[16,32]{1,0:T(8,128)S(1)}, f32[16,32]{1,0:T(8,128)S(1)}) all-reduce(f32[16,32]{1,0:T(8,128)S(1)} %get-tuple-element.6, f32[16,32]{1,0:T(8,128)S(1)} %get-tuple-element.5), channel_id=1, replica_groups=mesh['dp'=8,'ta'=16,'ha'=4] {'ha'}, use_global_device_ids=true, to_apply=%region_8.9 | all-reduce | flops 1024 | bytes 8192 | tf_op jit(solution)/shard_map/psum | solution.py:47
  49.9 2.4 %collective-permute-start = (bf16[2,4,2,384]{3,0,2,1:T(2,128)(2,1)S(1)}, bf16[2,4,2,384]{3,0,2,1:T(2,128)(2,1)S(1)}, u32[]{:S(2)}, u32[]{:S(2)}) collective-permute-start(bf16[2,4,2,384]{3,0,2,1:T(2,128)(2,1)S(1)} %slice.119), channel_id=1, source_target_pairs={{0,4},{4,8},{8,12},{12,16},{16,20},{20,24},{24,28},{28,32},{32,36}... | collective-permute-start | bytes 36872 | tf_op jit(solution)/shard_map/ppermute | solution.py:16
  52.4 2.9 %copy.55 = bf16[3,384,3,3,96]{1,0,4,3,2:T(4,128)(2,1)S(1)} copy(bf16[3,384,3,3,96]{1,4,3,2,0:T(8,128)(2,1)} %bitcast.90) | data formatting | bytes 3981312 | tf_op jit(solution)/shard_map/transpose | solution.py:65
  55.3 0.4 copy.67
  55.7 0.8 dynamic_slice.10
  56.5 1.2 collective-permute-done
  57.8 11.8 %all_gather.6 = bf16[18,16,2,384]{3,2,0,1:T(2,128)(2,1)S(1)} all-gather(bf16[18,4,2,384]{3,2,0,1:T(2,128)(2,1)S(1)} %copy.53), channel_id=1, replica_groups=mesh['dp'=8,'ta'=16,'ha'=4] {'ha'}, dimensions={1}, use_global_device_ids=true | all-gather | bytes 552960 | tf_op jit(solution)/shard_map/all_gather | solution.py:42
  69.6 0.4 fusion.10
  70.0 5.5 %fusion = f32[16,18,4,9,96]{4,1,3,2,0:T(8,128)S(1)} fusion(bf16[9,96,1152,1,1]{2,1,0,4,3:T(8,128)(2,1)S(1)} %bitcast.92, bf16[16,18,4,384]{3,1,2,0:T(8,128)(2,1)S(1)} %get-tuple-element.22, bf16[16,18,4,384]{3,1,2,0:T(8,128)(2,1)S(1)} %get-tuple-element.21, bf16[16,18,4,384]{3,1,2,0:T(8,128)(2,1)S(1)} %get-tuple-element.20), kind=kOutput, calls=%fused_computation.1 | convolution fusion | flops 2301198336 | bytes 8626176 | tf_op jit(solution)/shard_map/dot_general | solution.py:66
  75.8 12.6 %all_to_all.32 = bf16[16,16,2,96]{3,2,0,1:T(2,128)(2,1)S(1)} all-to-all(bf16[16,16,2,96]{3,2,0,1:T(2,128)(2,1)S(1)} %copy.56), channel_id=1, replica_groups=mesh['dp'=8,'ta'=16,'ha'=4] {'ha'}, dimensions={1} | all-to-all | bytes 196608 | tf_op jit(solution)/shard_map/all_to_all | solution.py:164
  88.6 0.3 fusion.43
  89.6 18.0 %all-reduce.2 = (f32[16,32]{1,0:T(8,128)S(1)}, f32[16,32]{1,0:T(8,128)S(1)}) all-reduce(f32[16,32]{1,0:T(8,128)S(1)} %reduce_sum.103, f32[16,32]{1,0:T(8,128)S(1)} %reduce_sum.100), channel_id=1, replica_groups=mesh['dp'=8,'ta'=16,'ha'=4] {'ha'}, use_global_device_ids=true, to_apply=%region_16.17 | all-reduce | flops 1024 | bytes 8192 | tf_op jit(solution)/shard_map/psum | solution.py:47
  108.5 1.9 %collective-permute-start.1 = (bf16[2,4,2,384]{3,0,2,1:T(2,128)(2,1)S(1)}, bf16[2,4,2,384]{3,0,2,1:T(2,128)(2,1)S(1)}, u32[]{:S(2)}, u32[]{:S(2)}) collective-permute-start(bf16[2,4,2,384]{3,0,2,1:T(2,128)(2,1)S(1)} %slice.129), channel_id=1, source_target_pairs={{0,4},{4,8},{8,12},{12,16},{16,20},{20,24},{24,28},{28,32},{32,36}... | collective-permute-start | bytes 36872 | tf_op jit(solution)/shard_map/ppermute | solution.py:16
  110.4 1.4 copy.60
  111.8 0.4 copy.68
  112.2 0.8 dynamic_slice.11
  112.9 3.2 %collective-permute-done.1 = bf16[2,4,2,384]{3,0,2,1:T(2,128)(2,1)S(1)} collective-permute-done((bf16[2,4,2,384]{3,0,2,1:T(2,128)(2,1)S(1)}, bf16[2,4,2,384]{3,0,2,1:T(2,128)(2,1)S(1)}, u32[]{:S(2)}, u32[]{:S(2)}) %collective-permute-start.1) | collective-permute-done | bytes 12320 | tf_op jit(solution)/shard_map/ppermute | solution.py:16
  116.3 12.8 %all_gather.7 = bf16[18,16,2,384]{3,2,0,1:T(2,128)(2,1)S(1)} all-gather(bf16[18,4,2,384]{3,2,0,1:T(2,128)(2,1)S(1)} %copy.58), channel_id=1, replica_groups=mesh['dp'=8,'ta'=16,'ha'=4] {'ha'}, dimensions={1}, use_global_device_ids=true | all-gather | bytes 552960 | tf_op jit(solution)/shard_map/all_gather | solution.py:42
  129.2 0.4 fusion.13
  129.6 5.4 %fusion.5 = f32[16,18,4,9,96]{4,1,3,2,0:T(8,128)S(1)} fusion(bf16[9,96,1152,1,1]{2,1,0,4,3:T(8,128)(2,1)S(1)} %bitcast.93, bf16[16,18,4,384]{3,1,2,0:T(8,128)(2,1)S(1)} %get-tuple-element.19, bf16[16,18,4,384]{3,1,2,0:T(8,128)(2,1)S(1)} %get-tuple-element.18, bf16[16,18,4,384]{3,1,2,0:T(8,128)(2,1)S(1)} %get-tuple-element.17), kind=kOutput, calls=%fused_computation.7 | convolution fusion | flops 2301198336 | bytes 8626176 | tf_op jit(solution)/shard_map/dot_general | solution.py:66
  135.3 16.3 %all_to_all.33 = f32[16,16,2,96]{3,2,0,1:T(2,128)S(1)} all-to-all(f32[16,16,2,96]{3,2,0,1:T(2,128)S(1)} %copy.61), channel_id=1, replica_groups=mesh['dp'=8,'ta'=16,'ha'=4] {'ha'}, dimensions={1} | all-to-all | bytes 393216 | tf_op jit(solution)/shard_map/all_to_all | solution.py:172
  151.7 0.3 all_to_all.28
  152.1 0.7 add_convert_fusion
  (63 shorter events, 5.0 us)
Async XLA Ops:
  0.0 1.3 copy-start
  2.2 24.7 %all-to-all-start = ((bf16[64,2,768]{2,1,0:T(2,128)(2,1)}), bf16[64,2,768]{2,1,0:T(2,128)(2,1)S(1)}, u32[]{:S(2)}, u32[]{:S(2)}) async-start(bf16[64,2,768]{2,1,0:T(2,128)(2,1)} %reshape.351), calls=%async_computation | async-start | bytes 393216 | tf_op jit(solution)/shard_map/all_to_all | solution.py:106
  29.5 20.3 %copy-start.2 = (f32[384]{0:T(512)S(1)}, f32[384]{0:T(512)}, u32[]{:S(2)}) copy-start(f32[384]{0:T(512)} %param.15) | copy-start | bytes 4612
  29.5 20.3 %copy-start.3 = (f32[384]{0:T(512)S(1)}, f32[384]{0:T(512)}, u32[]{:S(2)}) copy-start(f32[384]{0:T(512)} %param.14) | copy-start | bytes 4612
  49.9 7.7 %collective-permute-start = (bf16[2,4,2,384]{3,0,2,1:T(2,128)(2,1)S(1)}, bf16[2,4,2,384]{3,0,2,1:T(2,128)(2,1)S(1)}, u32[]{:S(2)}, u32[]{:S(2)}) collective-permute-start(bf16[2,4,2,384]{3,0,2,1:T(2,128)(2,1)S(1)} %slice.119), channel_id=1, source_target_pairs={{0,4},{4,8},{8,12},{12,16},{16,20},{20,24},{24,28},{28,32},{32,36}... | collective-permute-start | bytes 36872 | tf_op jit(solution)/shard_map/ppermute | solution.py:16
  88.4 19.9 %copy-start.4 = (f32[384]{0:T(512)S(1)}, f32[384]{0:T(512)}, u32[]{:S(2)}) copy-start(f32[384]{0:T(512)} %param.19) | copy-start | bytes 4612
  88.4 19.9 %copy-start.5 = (f32[384]{0:T(512)S(1)}, f32[384]{0:T(512)}, u32[]{:S(2)}) copy-start(f32[384]{0:T(512)} %param.18) | copy-start | bytes 4612
  88.6 21.8 %copy-start.1 = (bf16[3,3,3,96,384]{4,3,2,1,0:T(8,128)(2,1)S(1)}, bf16[3,3,3,96,384]{4,3,2,1,0:T(8,128)(2,1)}, u32[]{:S(2)}) copy-start(bf16[3,3,3,96,384]{4,3,2,1,0:T(8,128)(2,1)} %param.20) | copy-start | bytes 5971972
  108.5 7.7 %collective-permute-start.1 = (bf16[2,4,2,384]{3,0,2,1:T(2,128)(2,1)S(1)}, bf16[2,4,2,384]{3,0,2,1:T(2,128)(2,1)S(1)}, u32[]{:S(2)}, u32[]{:S(2)}) collective-permute-start(bf16[2,4,2,384]{3,0,2,1:T(2,128)(2,1)S(1)} %slice.129), channel_id=1, source_target_pairs={{0,4},{4,8},{8,12},{12,16},{16,20},{20,24},{24,28},{28,32},{32,36}... | collective-permute-start | bytes 36872 | tf_op jit(solution)/shard_map/ppermute | solution.py:16
where the time goes:
time: 153 us
  blocking collectives  90.5 us (59%)
  starting transfers between devices  17.4 us (11%)
  waiting for transfers between devices  13.8 us (9%)
  local copies, waits for them, and re-layouts  13.7 us (9%)
  matrix products  11.2 us (7%)
  other arithmetic  5.8 us (4%)
    psum x2, blocking collectives, shared_norm(): totals, squares = lax.psum((part_sums, part_squares), 'ha')  37 us
    all_gather x2, blocking collectives, whole_rows(): return lax.all_gather(values, 'ha', axis=1, tiled=True)  24.6 us
    all_to_all x1, blocking collectives, local(): lax.all_to_all(result, 'ha', split_axis=1, concat_axis=3, tiled=True)  16.3 us
    all_to_all x1, starting transfers between devices, rearrange_rows(): lax.all_to_all(departing_rows.reshape(devices, capacity, -1), ('ta', 'ha'...  13 us
    all_to_all x1, blocking collectives, local(): lax.all_to_all(hidden, 'ha', split_axis=1, concat_axis=3, tiled=True)  12.6 us
    dot_general x2, matrix products, causal_conv(): jnp.dot(stacked.reshape(-1, 3 * channels), kernel, preferred_element_type...  10.8 us
    all_to_all x1, waiting for transfers between devices, rearrange_rows(): lax.all_to_all(departing_rows.reshape(devices, capacity, -1), ('ta', 'ha'...  9.42 us
    ppermute x2, waiting for transfers between devices, from_behind(): return lax.ppermute(value, axis, pairs)  4.42 us
  transfers between devices with their start and end apart: 3, of which 3 were waited for; matrix products, arithmetic and copies ran while one was open for 6% of the time, Pallas kernels for 0%

commit v1 on v0

--- a/solution.py
+++ b/solution.py
@@ -39,7 +39,9 @@
 
 
 def whole_rows(values):
-    return lax.all_gather(values, "ha", axis=1, tiled=True)
+    return jnp.concatenate(
+        lax.all_to_all(jnp.stack([values] * lax.axis_size("ha")), "ha", 0, 0), axis=1
+    )
 
 
 def shared_norm(values, gain_vec, offset, entries):

time: 153 us -> 174 us (1.14)
  waiting for transfers between devices: 13.8 us -> 46.4 us
  blocking collectives: 90.5 us -> 64.6 us
  starting transfers between devices: 17.4 us -> 29.3 us
  local copies, waits for them, and re-layouts: 13.7 us -> 16 us
    all_to_all x0 -> x2, waiting for transfers between devices: none -> 28.6 us  [whole_rows(): lax.all_to_all(jnp.stack([values] * lax.axis_size('ha')), 'ha', 0, 0)]
    all_gather x2 -> x0, blocking collectives: 24.6 us -> none  [whole_rows(): return lax.all_gather(values, 'ha', axis=1, tiled=True)]
    all_to_all x0 -> x2, starting transfers between devices: none -> 11.9 us  [whole_rows(): lax.all_to_all(jnp.stack([values] * lax.axis_size('ha')), 'ha', 0, 0)]
    ppermute x2, waiting for transfers between devices: 4.42 us -> 6.76 us  [from_behind(): return lax.ppermute(value, axis, pairs)]
    another operation x0 -> x2, local copies, waits for them, and re-layouts: none -> 1.77 us  [whole_rows(): jnp.stack([values] * lax.axis_size('ha'))]
  transfers between devices with their start and end apart: 3 -> 5, of which waited for: 3 -> 5; matrix products, arithmetic and copies ran while one was open for 6% -> 4% of each run, Pallas kernels for 0% -> 0%
where the time goes in v1:
time: 174 us; the launch traced here: 173 us
  blocking collectives  64.6 us (37%)
  waiting for transfers between devices  46.4 us (27%)
  starting transfers between devices  29.3 us (17%)
  local copies, waits for them, and re-layouts  16 us (9%)
  matrix products  11.3 us (6%)
  other arithmetic  5.23 us (3%)
    psum x2, blocking collectives, shared_norm(): totals, squares = lax.psum((part_sums, part_squares), 'ha')  37.1 us
    all_to_all x2, waiting for transfers between devices, whole_rows(): lax.all_to_all(jnp.stack([values] * lax.axis_size('ha')), 'ha', 0, 0)  28.6 us
    all_to_all x1, blocking collectives, local(): lax.all_to_all(result, 'ha', split_axis=1, concat_axis=3, tiled=True)  15.1 us
    all_to_all x1, starting transfers between devices, rearrange_rows(): lax.all_to_all(departing_rows.reshape(devices, capacity, -1), ('ta', 'ha'...  13 us
    all_to_all x1, blocking collectives, local(): lax.all_to_all(hidden, 'ha', split_axis=1, concat_axis=3, tiled=True)  12.3 us
    all_to_all x2, starting transfers between devices, whole_rows(): lax.all_to_all(jnp.stack([values] * lax.axis_size('ha')), 'ha', 0, 0)  11.9 us
    all_to_all x1, waiting for transfers between devices, rearrange_rows(): lax.all_to_all(departing_rows.reshape(devices, capacity, -1), ('ta', 'ha'...  11 us
    dot_general x2, matrix products, causal_conv(): jnp.dot(stacked.reshape(-1, 3 * channels), kernel, preferred_element_type...  10.9 us
  transfers between devices with their start and end apart: 5, of which 5 were waited for; matrix products, arithmetic and copies ran while one was open for 4% of the time, Pallas kernels for 0%

profile of v1, /device:TPU:112, one launch (start us, length us, event | category | flops | bytes accessed | tf_op | source)
XLA Modules:
  0.0 173.2 jit_solution(14138129364510027681)
XLA Ops:
  0.0 0.8 reshape.366
  1.5 0.8 reshape.367
  2.2 13.0 %all-to-all-start = ((bf16[64,2,768]{2,1,0:T(2,128)(2,1)}), bf16[64,2,768]{2,1,0:T(2,128)(2,1)S(1)}, u32[]{:S(2)}, u32[]{:S(2)}) async-start(bf16[64,2,768]{2,1,0:T(2,128)(2,1)} %reshape.367), calls=%async_computation | async-start | bytes 393216 | tf_op jit(solution)/shard_map/all_to_all | solution.py:108
  15.9 11.0 %all-to-all-done = bf16[64,2,768]{2,1,0:T(2,128)(2,1)S(1)} async-done(((bf16[64,2,768]{2,1,0:T(2,128)(2,1)}), bf16[64,2,768]{2,1,0:T(2,128)(2,1)S(1)}, u32[]{:S(2)}, u32[]{:S(2)}) %all-to-all-start) | async-done | bytes 196640 | tf_op jit(solution)/shard_map/all_to_all | solution.py:108
  27.2 2.3 %reshape.378 = f32[16,8,32,12]{3,2,1,0:T(8,128)S(1)} reshape(f32[64,768]{1,0:T(8,128)S(1)} %fusion.16) | data formatting | bytes 393216 | tf_op jit(solution)/shard_map/convert_element_type | solution.py:160
  29.7 0.4 fusion.43
  30.1 19.1 %all-reduce.3 = (f32[16,32]{1,0:T(8,128)S(1)}, f32[16,32]{1,0:T(8,128)S(1)}) all-reduce(f32[16,32]{1,0:T(8,128)S(1)} %get-tuple-element.6, f32[16,32]{1,0:T(8,128)S(1)} %get-tuple-element.5), channel_id=1, replica_groups=mesh['dp'=8,'ta'=16,'ha'=4] {'ha'}, use_global_device_ids=true, to_apply=%region_8.9 | all-reduce | flops 1024 | bytes 8192 | tf_op jit(solution)/shard_map/psum | solution.py:49
  50.1 2.4 %collective-permute-start = (bf16[2,4,2,384]{3,2,1,0:T(2,128)(2,1)S(1)}, bf16[2,4,2,384]{3,2,1,0:T(2,128)(2,1)S(1)}, u32[]{:S(2)}, u32[]{:S(2)}) collective-permute-start(bf16[2,4,2,384]{3,2,1,0:T(2,128)(2,1)S(1)} %slice.119), channel_id=1, source_target_pairs={{0,4},{4,8},{8,12},{12,16},{16,20},{20,24},{24,28},{28,32},{32,36}... | collective-permute-start | bytes 36872 | tf_op jit(solution)/shard_map/ppermute | solution.py:16
  52.8 2.9 %copy.47 = bf16[3,384,3,3,96]{1,0,4,3,2:T(4,128)(2,1)S(1)} copy(bf16[3,384,3,3,96]{1,4,3,2,0:T(8,128)(2,1)} %bitcast.92) | data formatting | bytes 3981312 | tf_op jit(solution)/shard_map/transpose | solution.py:67
  55.7 0.4 copy.61
  56.1 0.8 dynamic_slice.10
  56.8 1.0 collective-permute-done
  58.0 0.9 stack.6
  58.9 5.3 %all-to-all-start.1 = ((bf16[4,18,4,2,384]{4,2,3,1,0:T(4,128)(2,1)}), bf16[4,18,4,2,384]{4,2,3,1,0:T(4,128)(2,1)S(1)}, u32[]{:S(2)}, u32[]{:S(2)}) async-start(bf16[4,18,4,2,384]{4,2,3,1,0:T(4,128)(2,1)} %stack.6), calls=%async_computation.1 | async-start | bytes 884736 | tf_op jit(solution)/shard_map/all_to_all | solution.py:43
  64.3 16.4 %all-to-all-done.1 = bf16[4,18,4,2,384]{4,2,3,1,0:T(4,128)(2,1)S(1)} async-done(((bf16[4,18,4,2,384]{4,2,3,1,0:T(4,128)(2,1)}), bf16[4,18,4,2,384]{4,2,3,1,0:T(4,128)(2,1)S(1)}, u32[]{:S(2)}, u32[]{:S(2)}) %all-to-all-start.1) | async-done | bytes 442400 | tf_op jit(solution)/shard_map/all_to_all | solution.py:43
  81.0 0.4 fusion.10
  81.4 5.5 %fusion = f32[16,18,4,9,96]{4,1,3,2,0:T(8,128)S(1)} fusion(bf16[9,96,1152,1,1]{2,1,0,4,3:T(8,128)(2,1)S(1)} %bitcast.94, bf16[16,18,4,384]{3,1,2,0:T(8,128)(2,1)S(1)} %get-tuple-element.22, bf16[16,18,4,384]{3,1,2,0:T(8,128)(2,1)S(1)} %get-tuple-element.21, bf16[16,18,4,384]{3,1,2,0:T(8,128)(2,1)S(1)} %get-tuple-element.20), kind=kOutput, calls=%fused_computation.1 | convolution fusion | flops 2301198336 | bytes 8626176 | tf_op jit(solution)/shard_map/dot_general | solution.py:68
  87.2 12.3 %all_to_all.42 = bf16[16,16,2,96]{3,2,0,1:T(2,128)(2,1)S(1)} all-to-all(bf16[16,16,2,96]{3,2,0,1:T(2,128)(2,1)S(1)} %copy.48), channel_id=1, replica_groups=mesh['dp'=8,'ta'=16,'ha'=4] {'ha'}, dimensions={1} | all-to-all | bytes 196608 | tf_op jit(solution)/shard_map/all_to_all | solution.py:166
  99.5 0.4 fusion.24
  100.5 18.1 %all-reduce.2 = (f32[16,32]{1,0:T(8,128)S(1)}, f32[16,32]{1,0:T(8,128)S(1)}) all-reduce(f32[16,32]{1,0:T(8,128)S(1)} %reduce_sum.103, f32[16,32]{1,0:T(8,128)S(1)} %reduce_sum.100), channel_id=1, replica_groups=mesh['dp'=8,'ta'=16,'ha'=4] {'ha'}, use_global_device_ids=true, to_apply=%region_16.17 | all-reduce | flops 1024 | bytes 8192 | tf_op jit(solution)/shard_map/psum | solution.py:49
  120.2 1.9 %collective-permute-start.1 = (bf16[2,4,2,384]{3,2,1,0:T(2,128)(2,1)S(1)}, bf16[2,4,2,384]{3,2,1,0:T(2,128)(2,1)S(1)}, u32[]{:S(2)}, u32[]{:S(2)}) collective-permute-start(bf16[2,4,2,384]{3,2,1,0:T(2,128)(2,1)S(1)} %slice.129), channel_id=1, source_target_pairs={{0,4},{4,8},{8,12},{12,16},{16,20},{20,24},{24,28},{28,32},{32,36}... | collective-permute-start | bytes 36872 | tf_op jit(solution)/shard_map/ppermute | solution.py:16
  122.1 5.8 %collective-permute-done.1 = bf16[2,4,2,384]{3,2,1,0:T(2,128)(2,1)S(1)} collective-permute-done((bf16[2,4,2,384]{3,2,1,0:T(2,128)(2,1)S(1)}, bf16[2,4,2,384]{3,2,1,0:T(2,128)(2,1)S(1)}, u32[]{:S(2)}, u32[]{:S(2)}) %collective-permute-start.1) | collective-permute-done | bytes 12320 | tf_op jit(solution)/shard_map/ppermute | solution.py:16
  128.1 0.9 stack.8
  129.0 6.7 %all-to-all-start.3 = ((bf16[4,18,4,2,384]{4,2,3,1,0:T(4,128)(2,1)}), bf16[4,18,4,2,384]{4,2,3,1,0:T(4,128)(2,1)S(1)}, u32[]{:S(2)}, u32[]{:S(2)}) async-start(bf16[4,18,4,2,384]{4,2,3,1,0:T(4,128)(2,1)} %stack.8), calls=%async_computation.3 | async-start | bytes 884736 | tf_op jit(solution)/shard_map/all_to_all | solution.py:43
  135.6 1.4 copy.54
  137.0 0.4 copy.62
  137.4 0.8 dynamic_slice.11
  138.1 12.2 %all-to-all-done.3 = bf16[4,18,4,2,384]{4,2,3,1,0:T(4,128)(2,1)S(1)} async-done(((bf16[4,18,4,2,384]{4,2,3,1,0:T(4,128)(2,1)}), bf16[4,18,4,2,384]{4,2,3,1,0:T(4,128)(2,1)S(1)}, u32[]{:S(2)}, u32[]{:S(2)}) %all-to-all-start.3) | async-done | bytes 442400 | tf_op jit(solution)/shard_map/all_to_all | solution.py:43
  150.6 0.4 fusion.13
  151.0 5.5 %fusion.5 = f32[16,18,4,9,96]{4,1,3,2,0:T(8,128)S(1)} fusion(bf16[9,96,1152,1,1]{2,1,0,4,3:T(8,128)(2,1)S(1)} %bitcast.95, bf16[16,18,4,384]{3,1,2,0:T(8,128)(2,1)S(1)} %get-tuple-element.19, bf16[16,18,4,384]{3,1,2,0:T(8,128)(2,1)S(1)} %get-tuple-element.18, bf16[16,18,4,384]{3,1,2,0:T(8,128)(2,1)S(1)} %get-tuple-element.17), kind=kOutput, calls=%fused_computation.7 | convolution fusion | flops 2301198336 | bytes 8626176 | tf_op jit(solution)/shard_map/dot_general | solution.py:68
  156.8 15.1 %all_to_all.43 = f32[16,16,2,96]{3,2,0,1:T(2,128)S(1)} all-to-all(f32[16,16,2,96]{3,2,0,1:T(2,128)S(1)} %copy.55), channel_id=1, replica_groups=mesh['dp'=8,'ta'=16,'ha'=4] {'ha'}, dimensions={1} | all-to-all | bytes 393216 | tf_op jit(solution)/shard_map/all_to_all | solution.py:174
  172.5 0.8 add_convert_fusion
  (73 shorter events, 7.0 us)
Async XLA Ops:
  0.0 1.3 copy-start
  2.2 24.7 %all-to-all-start = ((bf16[64,2,768]{2,1,0:T(2,128)(2,1)}), bf16[64,2,768]{2,1,0:T(2,128)(2,1)S(1)}, u32[]{:S(2)}, u32[]{:S(2)}) async-start(bf16[64,2,768]{2,1,0:T(2,128)(2,1)} %reshape.367), calls=%async_computation | async-start | bytes 393216 | tf_op jit(solution)/shard_map/all_to_all | solution.py:108
  29.5 20.3 %copy-start.2 = (f32[384]{0:T(512)S(1)}, f32[384]{0:T(512)}, u32[]{:S(2)}) copy-start(f32[384]{0:T(512)} %param.15) | copy-start | bytes 4612
  29.5 20.3 %copy-start.3 = (f32[384]{0:T(512)S(1)}, f32[384]{0:T(512)}, u32[]{:S(2)}) copy-start(f32[384]{0:T(512)} %param.14) | copy-start | bytes 4612
  29.6 23.0 %copy-start.6 = (s32[6]{0:T(128)S(1)}, s32[6]{0:T(128)}, u32[]{:S(2)}) copy-start(s32[6]{0:T(128)} %param.13) | copy-start | bytes 76
  50.1 7.7 %collective-permute-start = (bf16[2,4,2,384]{3,2,1,0:T(2,128)(2,1)S(1)}, bf16[2,4,2,384]{3,2,1,0:T(2,128)(2,1)S(1)}, u32[]{:S(2)}, u32[]{:S(2)}) collective-permute-start(bf16[2,4,2,384]{3,2,1,0:T(2,128)(2,1)S(1)} %slice.119), channel_id=1, source_target_pairs={{0,4},{4,8},{8,12},{12,16},{16,20},{20,24},{24,28},{28,32},{32,36}... | collective-permute-start | bytes 36872 | tf_op jit(solution)/shard_map/ppermute | solution.py:16
  58.9 21.8 %all-to-all-start.1 = ((bf16[4,18,4,2,384]{4,2,3,1,0:T(4,128)(2,1)}), bf16[4,18,4,2,384]{4,2,3,1,0:T(4,128)(2,1)S(1)}, u32[]{:S(2)}, u32[]{:S(2)}) async-start(bf16[4,18,4,2,384]{4,2,3,1,0:T(4,128)(2,1)} %stack.6), calls=%async_computation.1 | async-start | bytes 884736 | tf_op jit(solution)/shard_map/all_to_all | solution.py:43
  99.5 20.3 %copy-start.4 = (f32[384]{0:T(512)S(1)}, f32[384]{0:T(512)}, u32[]{:S(2)}) copy-start(f32[384]{0:T(512)} %param.19) | copy-start | bytes 4612
  99.5 20.4 %copy-start.5 = (f32[384]{0:T(512)S(1)}, f32[384]{0:T(512)}, u32[]{:S(2)}) copy-start(f32[384]{0:T(512)} %param.18) | copy-start | bytes 4612
  119.0 16.6 %copy-start.1 = (bf16[3,3,3,96,384]{4,3,2,1,0:T(8,128)(2,1)S(1)}, bf16[3,3,3,96,384]{4,3,2,1,0:T(8,128)(2,1)}, u32[]{:S(2)}) copy-start(bf16[3,3,3,96,384]{4,3,2,1,0:T(8,128)(2,1)} %param.20) | copy-start | bytes 5971972
  120.2 7.7 %collective-permute-start.1 = (bf16[2,4,2,384]{3,2,1,0:T(2,128)(2,1)S(1)}, bf16[2,4,2,384]{3,2,1,0:T(2,128)(2,1)S(1)}, u32[]{:S(2)}, u32[]{:S(2)}) collective-permute-start(bf16[2,4,2,384]{3,2,1,0:T(2,128)(2,1)S(1)} %slice.129), channel_id=1, source_target_pairs={{0,4},{4,8},{8,12},{12,16},{16,20},{20,24},{24,28},{28,32},{32,36}... | collective-permute-start | bytes 36872 | tf_op jit(solution)/shard_map/ppermute | solution.py:16
  129.0 21.3 %all-to-all-start.3 = ((bf16[4,18,4,2,384]{4,2,3,1,0:T(4,128)(2,1)}), bf16[4,18,4,2,384]{4,2,3,1,0:T(4,128)(2,1)S(1)}, u32[]{:S(2)}, u32[]{:S(2)}) async-start(bf16[4,18,4,2,384]{4,2,3,1,0:T(4,128)(2,1)} %stack.8), calls=%async_computation.3 | async-start | bytes 884736 | tf_op jit(solution)/shard_map/all_to_all | solution.py:43
